TPU v7x, 128 devices: a whole 4x4x4 slice. The times are simulated.
128 devices in a mesh: dp: 4 (over y), expert: 32 (over z, x, core).
Axes of the slice: x: 4, y: 4, z: 4, core: 2. Of those that a mesh axis runs over, the one named last changes fastest.
Arguments:
- grad_out: bfloat16 [32768, 4096], P(('dp', 'expert')), may hold values from -6 to 6
- expert_ids: int32 [32768, 8], P(('dp', 'expert')), may hold values from 0 to 63, all different within a row; in each aligned block of 256 rows (0 to 255, 256 to 511, ...) at most 36 rows name the same one
- route_weights: bfloat16 [32768, 8], P(('dp', 'expert')), may hold values from 0.099609375 to 1
- gate_values: bfloat16 [4, 64, 1152, 768], P('dp', 'expert'), may hold values from -5 to 5
- up_values: bfloat16 [4, 64, 1152, 768], P('dp', 'expert'), may hold values from -5 to 5
- w_down: bfloat16 [64, 768, 4096], P('expert', None, 'dp'), as said below
Outputs:
- grad_gate: bfloat16 [4, 64, 1152, 768], P('dp', 'expert')
- grad_up: bfloat16 [4, 64, 1152, 768], P('dp', 'expert')
- grad_down: bfloat16 [64, 768, 4096], P('expert', None, 'dp')
- grad_route: float32 [32768, 8], P(('dp', 'expert'))
Inputs may be any that keep to these rules, and one draw needn't show every extreme that they name: `expert_ids`: each token names 8 different experts. Among the tokens of one device no expert is named by more than 36 tokens, a bound that some block reaches. `w_down`: rows of the experts' weights and its columns have different scales.
All inputs are finite; a program needn't handle non-finite values.
Results may differ from a plain program's by a relative error of at most 0.015.
Values may be sent and summed in bfloat16 or wider, within the bound.
No kernel may reach another device: no remote copies, remote signals or barrier semaphores. Data moves between devices by JAX's collectives and lax.ppermute only.
A program may use at most 256 MiB of HBM per device.

v0:
```python
import jax
import jax.numpy as jnp
from jax import lax
from jax.sharding import PartitionSpec as P

epsilon = 1e-06


def shrink_groups(weight):
    dense_values = weight.astype(jnp.float32)
    block_count, hidden_units, column_total = dense_values.shape
    magnitude = jnp.abs(dense_values).reshape(block_count, hidden_units // 4, 4, column_total)
    lower_one = jnp.minimum(magnitude[:, :, 0], magnitude[:, :, 1])
    upper_one = jnp.maximum(magnitude[:, :, 0], magnitude[:, :, 1])
    lower_two = jnp.minimum(magnitude[:, :, 2], magnitude[:, :, 3])
    upper_two = jnp.maximum(magnitude[:, :, 2], magnitude[:, :, 3])
    second = jnp.minimum(jnp.maximum(lower_one, lower_two), jnp.minimum(upper_one, upper_two))
    kept_part = jnp.maximum(magnitude - second[:, :, None, :], 0.0).reshape(
        block_count, hidden_units, column_total
    )
    return (dense_values, jnp.sign(dense_values) * kept_part)


def route_table(expert_ids, expert_count, capacity):
    flat_ids = expert_ids.reshape(-1)
    onehot = (flat_ids[:, None] == jnp.arange(expert_count, dtype=jnp.int32)[None, :]).astype(
        jnp.int32
    )
    before = jnp.cumsum(onehot, axis=0) - onehot
    slot_index = jnp.sum(before * onehot, axis=1)
    return flat_ids * capacity + slot_index


def on_device(grad_out, expert_ids, route_weights, gate_values, up_values, w_down):
    group_count = lax.axis_size("expert")
    local_experts = gate_values.shape[1]
    slot_count = gate_values.shape[2]
    capacity = slot_count // group_count
    expert_count = local_experts * group_count
    top_count = expert_ids.shape[1]
    target_place = route_table(expert_ids, expert_count, capacity)
    row_count = target_place.shape[0]
    place_count = expert_count * capacity
    source_row = (
        jnp.zeros((place_count,), jnp.int32)
        .at[target_place]
        .set(jnp.arange(row_count, dtype=jnp.int32))
    )
    filled_mask = jnp.zeros((place_count,), jnp.int32).at[target_place].set(1) > 0
    send_rows = jnp.where(
        filled_mask[:, None], grad_out[source_row // top_count], jnp.zeros((), grad_out.dtype)
    )
    send_rows = send_rows.reshape(expert_count, capacity, grad_out.shape[1])
    send_weights = jnp.where(
        filled_mask, route_weights.reshape(-1)[source_row], jnp.zeros((), route_weights.dtype)
    )
    send_weights = send_weights.reshape(expert_count, capacity)
    arrived, slot_weights = (
        lax.all_to_all(send_rows, "expert", split_axis=0, concat_axis=1, tiled=True),
        lax.all_to_all(send_weights, "expert", split_axis=0, concat_axis=1, tiled=True),
    )
    dense_values, shrunk = shrink_groups(w_down)
    inner_sum, squares = lax.psum(
        (jnp.sum(dense_values * shrunk, axis=(1, 2)), jnp.sum(shrunk * shrunk, axis=(1, 2))), "dp"
    )
    factor = inner_sum / (squares + epsilon)
    effective = (factor[:, None, None] * shrunk).astype(jnp.bfloat16)
    slot_grads = jnp.einsum(
        "esd,ehd->esh",
        arrived,
        lax.all_gather(effective, "dp", axis=2, tiled=True),
        preferred_element_type=jnp.float32,
    )
    gate_float = gate_values[0].astype(jnp.float32)
    up_float = up_values[0].astype(jnp.float32)
    sigmoid_gate = jax.nn.sigmoid(gate_float)
    activated = gate_float * sigmoid_gate
    product = activated * up_float
    weight_float = slot_weights.astype(jnp.float32)
    scores = jnp.sum(slot_grads * product, axis=2)
    scaled = weight_float[:, :, None] * slot_grads
    grad_gate = (
        scaled * up_float * sigmoid_gate * (1.0 + gate_float * (1.0 - sigmoid_gate))
    ).astype(jnp.bfloat16)
    grad_up = (scaled * activated).astype(jnp.bfloat16)
    weighted = (weight_float[:, :, None] * product).astype(jnp.bfloat16)
    partial_grad = jnp.einsum("esh,esd->ehd", weighted, arrived, preferred_element_type=jnp.float32)
    summed = lax.psum_scatter(
        partial_grad.astype(jnp.bfloat16), "dp", scatter_dimension=2, tiled=True
    ).astype(jnp.float32)
    grad_down = (factor[:, None, None] * summed).astype(jnp.bfloat16)
    returned = lax.all_to_all(scores, "expert", split_axis=1, concat_axis=0, tiled=True)
    grad_route = returned.reshape(-1)[target_place].reshape(expert_ids.shape)
    return (grad_gate[None], grad_up[None], grad_down, grad_route)


def solution(mesh):
    in_specs = (
        P(("dp", "expert"), None),
        P(("dp", "expert"), None),
        P(("dp", "expert"), None),
        P("dp", "expert", None, None),
        P("dp", "expert", None, None),
        P("expert", None, "dp"),
    )
    out_specs = (
        P("dp", "expert", None, None),
        P("dp", "expert", None, None),
        P("expert", None, "dp"),
        P(("dp", "expert"), None),
    )
    return jax.shard_map(
        on_device, mesh=mesh, in_specs=in_specs, out_specs=out_specs, check_vma=False
    )
```

profile of v0, /device:TPU:1, one launch (start us, length us, event | category | flops | bytes accessed | tf_op | source)
XLA Modules:
  0.0 849.0 jit_solution(3353225667226428491)
XLA Ops:
  7.2 1.0 copy.47
  8.2 0.1 eq.29
  8.3 0.1 eq.25
  8.4 0.7 broadcast_multiply_fusion
  9.1 18.1 %reduce-window.6 = s32[64,16,128]{2,1,0:T(8,128)S(1)} reduce-window(s32[64,16,128]{2,1,0:T(8,128)S(1)} %fusion.23, s32[]{:T(128)} %constant.13.clone.1), window={size=1x1x128 pad=0_0x0_0x127_0}, to_apply=%region_0.0 | reduce-window | flops 16646144 | bytes 1048580 | tf_op jit(solution)/shard_map/reduce-window
  27.3 0.2 slice.34
  27.5 0.4 copy.63
  27.9 0.2 reduce-window.9
  28.1 0.2 broadcast_add_fusion
  28.3 0.1 copy.46
  28.4 0.1 mul.82
  28.6 0.3 fusion.22
  28.9 8.1 scatter_custom_fusion.1
  37.0 0.8 copy.51
  37.8 0.1 reshape.98
  37.9 8.1 scatter_custom_fusion
  46.0 13.9 %gather_fusion = bf16[2304]{0:T(1024)(128)(2,1)S(1)} fusion(bf16[2048]{0:T(1024)(128)(2,1)S(1)} %reshape.98, s32[3072]{0:T(1024)S(1)} %get-tuple-element.34), kind=kCustom, calls=%fused_computation | custom fusion | bytes 18432 | tf_op jit(solution)/shard_map/gather | solution.py:55
  59.9 0.7 all_to_all.35
  60.6 9.4 %all-to-all-start = ((bf16[32,2,36]{2,1,0:T(2,128)(2,1)}), bf16[32,2,36]{2,1,0:T(2,128)(2,1)S(1)}, u32[]{:S(2)}, u32[]{:S(2)}) async-start(bf16[32,2,36]{2,1,0:T(2,128)(2,1)} %all_to_all.35), calls=%async_computation | async-start | bytes 32768 | tf_op jit(solution)/shard_map/all_to_all | solution.py:60
  70.1 0.1 broadcast_in_dim.46
  70.2 13.5 %gather_fusion.1 = bf16[2304,4096]{1,0:T(8,128)(2,1)} fusion(bf16[256,4096]{1,0:T(8,128)(2,1)S(1)} %copy-done, s32[3072]{0:T(1024)S(1)} %get-tuple-element.33), kind=kCustom, calls=%fused_computation.1 | custom fusion | bytes 37757952 | tf_op jit(solution)/shard_map/gather | solution.py:51
  83.7 25.0 %gather.13 = bf16[64,36,4096]{2,1,0:T(8,128)(2,1)} reshape(bf16[2304,4096]{1,0:T(8,128)(2,1)} %gather_fusion.1) | data formatting | bytes 37748736 | tf_op jit(solution)/shard_map/gather | solution.py:51
  108.6 17.4 %broadcast_select_fusion = bf16[64,36,4096]{2,1,0:T(8,128)(2,1)} fusion(bf16[64,36,4096]{2,1,0:T(8,128)(2,1)} %gather.13, pred[64,36]{1,0:T(8,128)(4,1)S(1)} %broadcast_in_dim.46), kind=kLoop, calls=%fused_computation.5 | loop fusion | flops 9437184 | bytes 37751040 | tf_op jit(solution)/shard_map/jit(_where)/select_n | solution.py:50
  126.1 7.4 all-to-all-start.1
  133.6 5.7 copy.56
  139.3 5.7 copy.57
  145.2 241.2 %all-to-all-done.1 = bf16[64,36,4096]{2,1,0:T(8,128)(2,1)} async-done(((bf16[64,36,4096]{2,1,0:T(8,128)(2,1)}), bf16[64,36,4096]{2,1,0:T(8,128)(2,1)}, u32[]{:S(2)}, u32[]{:S(2)}) %all-to-all-start.1) | async-done | bytes 18874400 | tf_op jit(solution)/shard_map/all_to_all | solution.py:59
  386.4 34.3 %copy.65 = bf16[32,2,36,4096]{3,1,2,0:T(2,128)(2,1)} copy(bf16[32,2,36,4096]{3,2,1,0:T(8,128)(2,1)} %bitcast.6) | data formatting | bytes 37748736 | tf_op jit(solution)/shard_map/all_to_all | solution.py:59
  420.7 91.9 %fusion.4 = bf16[2,768,4096]{2,1,0:T(8,128)(2,1)} fusion(bf16[2,1152,4096]{2,0,1:T(2,128)(2,1)} %bitcast.61, bf16[1,2,1152,768]{2,3,1,0:T(8,128)(2,1)} %copy.56, f32[2,1152]{1,0:T(2,128)S(1)} %reshape.102, bf16[1,2,1152,768]{2,3,1,0:T(8,128)(2,1)} %copy.57), kind=kOutput, calls=%fused_computation.16 | convolution fusion | flops 14517731328 | bytes 38544384 | tf_op jit(solution)/shard_map/esh,esd->ehd/dot_general | solution.py:87
  512.7 5.4 convert_abs_fusion
  518.2 7.5 reshape.99
  525.6 12.8 %minimum_minimum_fusion = f32[2,192,1,1024]{3,2,1,0:T(1,128)S(1)} fusion(f32[2,192,4,1024]{3,2,1,0:T(4,128)} %reshape.99), kind=kLoop, calls=%fused_computation.39 | loop fusion | flops 2752512 | bytes 7864320 | tf_op jit(solution)/shard_map/min | solution.py:17
  538.4 0.3 copy.78
  538.8 4.5 sub.28
  543.3 7.7 sub.29
  550.9 7.8 multiply_reduce_fusion.1
  558.7 10.0 %all-reduce = (f32[2]{0:T(128)S(1)}, f32[2]{0:T(128)S(1)}) all-reduce(f32[2]{0:T(128)S(1)} %get-tuple-element.21, f32[2]{0:T(128)S(1)} %get-tuple-element.20), channel_id=1, replica_groups=mesh['dp'=4,'expert'=32] {'dp'}, use_global_device_ids=true, to_apply=%region_6.7 | all-reduce | flops 4 | bytes 32 | tf_op jit(solution)/shard_map/psum | solution.py:63
  568.8 69.9 %reduce-scatter.2.cloned.1.call-done = bf16[2,768,1024]{2,1,0:T(8,128)(2,1)} async-done(((bf16[2,768,4096]{2,1,0:T(8,128)(2,1)}), bf16[2,768,1024]{2,1,0:T(8,128)(2,1)}) %reduce-scatter.2.cloned.1.call-update) | async-done | bytes 3145744 | tf_op jit(solution)/shard_map/reduce_scatter | solution.py:88
  638.6 8.0 multiply_convert_fusion.2
  646.7 118.3 %all-gather.2.cloned.1.call-done = bf16[2,768,4096]{2,1,0:T(8,128)(2,1)} async-done(((bf16[2,768,1024]{2,1,0:T(8,128)(2,1)}), bf16[2,768,4096]{2,1,0:T(8,128)(2,1)}) %all-gather.2.cloned.1.call-update) | async-done | bytes 12582928 | tf_op jit(solution)/shard_map/all_gather | solution.py:71
  765.0 44.2 %multiply_reduce_fusion = (f32[2,1152]{1,0:T(2,128)S(1)}, bf16[1,2,1152,768]{2,3,1,0:T(8,128)(2,1)}, bf16[1,2,1152,768]{2,3,1,0:T(8,128)(2,1)}) fusion(bf16[1,2,1152,768]{2,3,1,0:T(8,128)(2,1)} %copy.56, bf16[1,2,1152,768]{2,3,1,0:T(8,128)(2,1)} %copy.57, f32[2,1152]{1,0:T(2,128)S(1)} %reshape.102, bf16[2,768,4096]{2,1,0:T(8,128)(2,1)} %all-gather.2.cloned.1.call-done, ...), kind=kOutput, calls=%fused_computation.26 | convolution fusion | flops 14529132544 | bytes 45631488 | tf_op jit(solution)/shard_map/esd,ehd->esh/dot_general | solution.py:68
  809.3 0.6 copy.59
  809.9 7.7 all-to-all-start.2
  817.6 5.8 copy.60
  823.4 5.9 copy.61
  829.3 0.1 reshape.100
  829.4 11.8 %gather_fusion.2 = f32[2048]{0:T(1024)S(1)} fusion(f32[2304]{0:T(1024)S(1)} %reshape.100, s32[2048]{0:T(1024)S(1)} %broadcast_clamp_fusion), kind=kCustom, calls=%fused_computation.2 | custom fusion | bytes 24576 | tf_op jit(solution)/shard_map/gather | solution.py:93
  841.3 0.7 copy.62
  (28 shorter events, 0.6 us)
Async XLA Ops:
  7.2 63.0 %copy-start = (bf16[256,4096]{1,0:T(8,128)(2,1)S(1)}, bf16[256,4096]{1,0:T(8,128)(2,1)}, u32[]{:S(2)}) copy-start(bf16[256,4096]{1,0:T(8,128)(2,1)} %param.6) | copy-start | bytes 6291460
  28.8 54.8 %copy-start.2 = (s32[2048,1]{0,1:T(1,128)}, s32[2048,1]{0,1:T(1,128)S(1)}, u32[]{:S(2)}) copy-start(s32[2048,1]{0,1:T(1,128)S(1)} %compare_select_fusion) | copy-start | bytes 24580
  60.6 65.5 %all-to-all-start = ((bf16[32,2,36]{2,1,0:T(2,128)(2,1)}), bf16[32,2,36]{2,1,0:T(2,128)(2,1)S(1)}, u32[]{:S(2)}, u32[]{:S(2)}) async-start(bf16[32,2,36]{2,1,0:T(2,128)(2,1)} %all_to_all.35), calls=%async_computation | async-start | bytes 32768 | tf_op jit(solution)/shard_map/all_to_all | solution.py:60
  126.1 260.3 %all-to-all-start.1 = ((bf16[64,36,4096]{2,1,0:T(8,128)(2,1)}), bf16[64,36,4096]{2,1,0:T(8,128)(2,1)}, u32[]{:S(2)}, u32[]{:S(2)}) async-start(bf16[64,36,4096]{2,1,0:T(8,128)(2,1)} %broadcast_select_fusion), calls=%async_computation.1 | async-start | bytes 41943040 | tf_op jit(solution)/shard_map/all_to_all | solution.py:59
  133.5 505.1 %reduce-scatter.2.cloned.1.call-start = ((), (), s32[]{:S(2)}) async-start(), calls=%async_computation.5 | async-start | bytes 15728640 | tf_op jit(solution)/shard_map/reduce_scatter | solution.py:88
  512.7 252.3 %all-gather.2.cloned.1.call-start = ((), (), s32[]{:S(2)}) async-start(), calls=%async_computation.4 | async-start | bytes 15728640 | tf_op jit(solution)/shard_map/all_gather | solution.py:71
  646.7 170.9 %copy-start.3 = (s32[2048,1]{0,1:T(1,128)S(1)}, s32[2048,1]{0,1:T(1,128)}, u32[]{:S(2)}) copy-start(s32[2048,1]{0,1:T(1,128)} %copy-done.2) | copy-start | bytes 24580
  809.9 19.4 %all-to-all-start.2 = ((f32[2,32,36]{2,0,1:T(2,128)}), f32[2,32,36]{2,0,1:T(2,128)S(1)}, u32[]{:S(2)}, u32[]{:S(2)}) async-start(f32[2,32,36]{2,0,1:T(2,128)} %copy.59), calls=%async_computation.3 | async-start | bytes 65536 | tf_op jit(solution)/shard_map/all_to_all | solution.py:92
  823.4 18.6 %copy-start.1 = (bf16[256,4096]{1,0:T(8,128)(2,1)S(1)}, bf16[256,4096]{1,0:T(8,128)(2,1)}, u32[]{:S(2)}) copy-start(bf16[256,4096]{1,0:T(8,128)(2,1)} %param.6) | copy-start | bytes 6291460
Sparse Core Ops, SparseCore 0:
  512.8 125.7 reduce-scatter.1
  646.8 118.1 all-gather.1
where the time goes:
time: 850 us; the launch traced here: 849 us
  waiting for transfers between devices  429 us (50%)
  local copies, waits for them, and re-layouts  163 us (19%)
  matrix products  136 us (16%)
  other arithmetic  71.1 us (8%)
  starting transfers between devices  24.6 us (3%)
  between operations  14.5 us (2%)
  blocking collectives  10 us (1%)
    all_to_all x1, waiting for transfers between devices, on_device(): lax.all_to_all(send_rows, 'expert', split_axis=0, concat_axis=1, tiled=True)  241 us
    all_gather x1, waiting for transfers between devices, on_device(): lax.all_gather(effective, 'dp', axis=2, tiled=True)  118 us
    dot_general x1, matrix products, on_device(): jnp.einsum('esh,esd->ehd', weighted, arrived, preferred_element_type=jnp....  91.9 us
    reduce_scatter x1, waiting for transfers between devices, on_device(): lax.psum_scatter(partial_grad.astype(jnp.bfloat16), 'dp', scatter_dimensi...  69.9 us
    dot_general x1, matrix products, on_device(): jnp.einsum('esd,ehd->esh', arrived, lax.all_gather(effective, 'dp', axis=...  44.2 us
    gather x2, local copies, waits for them, and re-layouts, on_device(): grad_out[source_row // top_count]  38.4 us
    all_to_all x1, local copies, waits for them, and re-layouts, on_device(): lax.all_to_all(send_rows, 'expert', split_axis=0, concat_axis=1, tiled=True)  34.3 us
    unnamed x16, local copies, waits for them, and re-layouts  26 us
  transfers between devices with their start and end apart: 5, of which 3 were waited for; matrix products, arithmetic and copies ran while one was open for 15% of the time, Pallas kernels for 0%

commit v1 on v0

v1 whole, which is shorter than its diff:
```python
import functools

import jax
import jax.numpy as jnp
from jax import lax
from jax.experimental import pallas as pl
from jax.experimental.pallas import tpu as pltpu
from jax.sharding import PartitionSpec as P

epsilon = 1e-06

D = 4096
H = 768
TOP = 8
TOK = 256
CAP = 36
SLOTS = 1152
NZ = NX = 4
NDP = 4
PART = 2 * CAP
SEG = NZ * PART
UNIT = 256
CHUNKS = 2
SHIFTS = (0, 1, 3, 2)
VMEM_LIMIT = 56 * 1024 * 1024


def member(z, x, core):
    return ((z % NZ) * NX + (x % NX)) * 2 + core


def pairs(first_axis, shift, swap):
    out = []
    for z in range(NZ):
        for x in range(NX):
            for core in range(2):
                along_z = (core == 0) == first_axis
                to = (z + shift, x) if along_z else (z, x + shift)
                out.append((member(z, x, core), member(*to, core ^ swap)))
    return out


def params(**kw):
    return pltpu.CompilerParams(vmem_limit_bytes=VMEM_LIMIT, **kw)


def cost(flops, nbytes, trans=0):
    return pl.CostEstimate(flops=int(flops), bytes_accessed=int(nbytes), transcendentals=int(trans))


def shrink_kernel(w_ref, out_ref, sums_ref):
    dense = w_ref[0].astype(jnp.float32)
    row = lax.broadcasted_iota(jnp.int32, dense.shape, 0)
    odd = (row & 1) == 1
    high = (row & 2) == 2

    def across(value, step, upper):
        return jnp.where(
            upper, pltpu.roll(value, step, 0), pltpu.roll(value, value.shape[0] - step, 0)
        )

    mag = jnp.abs(dense)
    other = across(mag, 1, odd)
    low, up = jnp.minimum(mag, other), jnp.maximum(mag, other)
    second = jnp.minimum(
        jnp.maximum(low, across(low, 2, high)), jnp.minimum(up, across(up, 2, high))
    )
    kept = jnp.maximum(mag - second, 0.0)
    shrunk = jnp.where(dense < 0.0, -kept, kept)
    out_ref[0, 0] = shrunk.astype(jnp.bfloat16)

    def fold(value):
        value = jnp.sum(value.reshape(H // 8, 8, UNIT), axis=0)
        return value[:, :128] + value[:, 128:]

    sums_ref[0, 0, 0] = fold(dense * shrunk)
    sums_ref[0, 0, 1] = fold(shrunk * shrunk)


def shrink(w_down):
    return pl.pallas_call(
        shrink_kernel,
        grid=(4, 2),
        in_specs=[pl.BlockSpec((1, H, UNIT), lambda q, e: (e, 0, q))],
        out_specs=[
            pl.BlockSpec((1, 1, H, UNIT), lambda q, e: (q, e, 0, 0)),
            pl.BlockSpec((1, 1, 2, 8, 128), lambda q, e: (q, e, 0, 0, 0)),
        ],
        out_shape=[
            jax.ShapeDtypeStruct((4, 2, H, UNIT), jnp.bfloat16),
            jax.ShapeDtypeStruct((4, 2, 2, 8, 128), jnp.float32),
        ],
        compiler_params=params(),
        cost_estimate=cost(2 * H * 1024 * 30, 2 * 2 * H * 1024 * 2),
        name="shrink",
    )(w_down)


def route_kernel(ids_ref, weights_ref, table_ref, rank_ref):
    expert = lax.broadcasted_iota(jnp.int32, (64, TOK), 0)
    named = jnp.zeros((64, TOK), jnp.float32)
    weight = jnp.zeros((64, TOK), jnp.float32)
    for k in range(TOP):
        hit = ids_ref[k : k + 1, :] == expert
        named = jnp.where(hit, 1.0, named)
        weight = jnp.where(hit, weights_ref[k : k + 1, :], weight)
    earlier = lax.broadcasted_iota(jnp.int32, (TOK, TOK), 0) < lax.broadcasted_iota(
        jnp.int32, (TOK, TOK), 1
    )
    rank = jnp.dot(
        named.astype(jnp.bfloat16),
        earlier.astype(jnp.bfloat16),
        preferred_element_type=jnp.float32,
    )
    rank = jnp.where(named > 0.0, rank, -1.0)
    rank_ref[...] = rank
    lane = lax.broadcasted_iota(jnp.int32, (64, 128), 1)
    slot_weight = jnp.zeros((64, 128), jnp.float32)
    for slot in range(CAP):
        one = jnp.sum(jnp.where(rank == float(slot), weight, 0.0), axis=1, keepdims=True)
        slot_weight = jnp.where(lane == slot, one, slot_weight)
    table_ref[:, :TOK] = rank.astype(jnp.bfloat16)
    table_ref[:, TOK:] = slot_weight.astype(jnp.bfloat16)


def route(ids, weights):
    return pl.pallas_call(
        route_kernel,
        out_shape=[
            jax.ShapeDtypeStruct((64, TOK + 128), jnp.bfloat16),
            jax.ShapeDtypeStruct((64, TOK), jnp.float32),
        ],
        compiler_params=params(),
        name="route",
    )(ids.T, weights.astype(jnp.float32).T)


def back_kernel(ids_ref, rank_ref, score_ref, out_ref):
    expert = lax.broadcasted_iota(jnp.int32, (64, TOK), 0)
    rank = rank_ref[...]
    score = jnp.zeros((64, TOK), jnp.float32)
    for slot in range(CAP):
        score = jnp.where(rank == float(slot), score_ref[:, slot : slot + 1], score)
    for k in range(TOP):
        hit = ids_ref[k : k + 1, :] == expert
        out_ref[k : k + 1, :] = jnp.sum(jnp.where(hit, score, 0.0), axis=0, keepdims=True)


def back(ids, rank, score):
    out = pl.pallas_call(
        back_kernel,
        out_shape=jax.ShapeDtypeStruct((TOP, TOK), jnp.float32),
        compiler_params=params(),
        name="back",
    )(ids.T, rank, score)
    return out.T


def pick_kernel(chunk, where_ref, rank_ref, *refs):
    blocks, outs = refs[:4], refs[4:12]
    tokens, onehot, picked, sems = refs[12:]
    step = pl.program_id(0)

    @pl.when(step == 0)
    def _():
        copies = [
            pltpu.make_async_copy(blocks[i].at[chunk], tokens.at[where_ref[i]], sems.at[i])
            for i in range(4)
        ]
        for copy in copies:
            copy.start()
        row = lax.broadcasted_iota(jnp.int32, (PART, 2 * TOK), 0)
        lane = lax.broadcasted_iota(jnp.int32, (PART, 2 * TOK), 1)
        second = row >= CAP
        slot = jnp.where(second, row - CAP, row)
        slot = jnp.where(second == (lane >= TOK), slot, -2).astype(jnp.float32)
        for block in range(4):
            for i in range(16):
                hit = slot == rank_ref[block, i : i + 1, :]
                onehot[block, i * PART : (i + 1) * PART, :] = jnp.where(hit, 1.0, 0.0).astype(
                    jnp.bfloat16
                )
        for copy in copies:
            copy.wait()

    columns = pl.ds(pl.multiple_of(step * UNIT, UNIT), UNIT)
    for block in range(4):
        picked[block] = jnp.dot(
            onehot[block], tokens[block, :, columns], preferred_element_type=jnp.float32
        )
    for i in range(16):
        rows = pl.ds(i * PART, PART)
        joined = jnp.concatenate([picked[block, rows, :] for block in range(4)], axis=0)
        outs[i // 2][i % 2] = joined.astype(jnp.bfloat16)


def pick(chunk, where, rank, blocks):
    any_spec = pl.BlockSpec(memory_space=pl.ANY)
    return pl.pallas_call(
        functools.partial(pick_kernel, chunk),
        grid_spec=pltpu.PrefetchScalarGridSpec(
            num_scalar_prefetch=1,
            grid=(4,),
            in_specs=[pl.BlockSpec((4, 16, 2 * TOK), lambda n, s: (0, 0, 0))] + [any_spec] * 4,
            out_specs=[pl.BlockSpec((2, SEG, UNIT), lambda n, s: (0, 0, n))] * 8,
            scratch_shapes=[
                pltpu.VMEM((4, 2 * TOK, 1024), jnp.bfloat16),
                pltpu.VMEM((4, 16 * PART, 2 * TOK), jnp.bfloat16),
                pltpu.VMEM((4, 16 * PART, UNIT), jnp.float32),
                pltpu.SemaphoreType.DMA((4,)),
            ],
        ),
        out_shape=[jax.ShapeDtypeStruct((2, SEG, 1024), jnp.bfloat16)] * 8,
        compiler_params=params(),
        cost_estimate=cost(2 * 4 * 1152 * 512 * 1024, 4 * 1024 * 1024 + 8 * 2 * SEG * 1024 * 2),
        name=f"pick{chunk}",
    )(where, rank, *blocks)


def weigh_kernel(gate_ref, up_ref, weight_ref, out_ref):
    gate = gate_ref[0].astype(jnp.float32)
    up = up_ref[0].astype(jnp.float32)
    sig = 1.0 / (1.0 + jnp.exp(-gate))
    value = weight_ref[0] * (gate * sig * up)
    out_ref[1, 0] = value.astype(jnp.bfloat16).T
    turned = jnp.concatenate(
        [
            value[(z * NX + x) * PART : (z * NX + x + 1) * PART]
            for x in range(NX)
            for z in range(NZ)
        ],
        axis=0,
    )
    out_ref[0, 0] = turned.astype(jnp.bfloat16).T


def weigh(gate, up, slot_weight):
    wide = 256
    return pl.pallas_call(
        weigh_kernel,
        grid=(2, H // wide),
        in_specs=[
            pl.BlockSpec((1, SLOTS, wide), lambda e, n: (e, 0, n)),
            pl.BlockSpec((1, SLOTS, wide), lambda e, n: (e, 0, n)),
            pl.BlockSpec((1, SLOTS, 1), lambda e, n: (e, 0, 0)),
        ],
        out_specs=pl.BlockSpec((2, 1, wide, SLOTS), lambda e, n: (0, e, n, 0)),
        out_shape=jax.ShapeDtypeStruct((2, 2, H, SLOTS), jnp.bfloat16),
        compiler_params=params(),
        cost_estimate=cost(2 * SLOTS * H * 20, 2 * SLOTS * H * 8, 2 * SLOTS * H),
        name="weigh",
    )(gate, up, slot_weight)


def row_copies(where_ref, buffers, group, e, rows, sems):
    return [
        pltpu.make_async_copy(
            buffers[4 * group + i].at[e],
            rows.at[pl.ds(pl.multiple_of(where_ref[4 * group + i] * SEG, SEG), SEG)],
            sems.at[i],
        )
        for i in range(4)
    ]


def partial_kernel(where_ref, weighted_ref, *refs):
    buffers, out_ref, rows, sems = refs[:8], refs[8], refs[9], refs[10]
    step = pl.program_id(0)
    slot = step & 1

    def fetch(at, into):
        for i in range(4):
            @pl.when(at == i)
            def _(i=i):
                for copy in row_copies(where_ref, buffers, i // 2, i % 2, rows.at[into], sems.at[into]):
                    copy.start()

    @pl.when(step == 0)
    def _():
        fetch(step, 0)

    @pl.when(step < 3)
    def _():
        fetch(step + 1, 1 - slot)

    for copy in row_copies(where_ref, buffers, 0, 0, rows.at[slot], sems.at[slot]):
        copy.wait()
    for j in range(NDP):
        out_ref[j, 0, 0] = jnp.dot(
            weighted_ref[0, 0],
            rows[slot, :, j * UNIT : (j + 1) * UNIT],
            preferred_element_type=jnp.float32,
        ).astype(jnp.bfloat16)


def partial(chunk, where, weighted, buffers):
    any_spec = pl.BlockSpec(memory_space=pl.ANY)
    return pl.pallas_call(
        partial_kernel,
        grid_spec=pltpu.PrefetchScalarGridSpec(
            num_scalar_prefetch=1,
            grid=(4,),
            in_specs=[pl.BlockSpec((1, 1, H, SLOTS), lambda n, s: (s[8 + n // 2], n % 2, 0, 0))]
            + [any_spec] * 8,
            out_specs=pl.BlockSpec(
                (NDP, 1, 1, H, UNIT), lambda n, s: (0, s[8 + n // 2], n % 2, 0, 0)
            ),
            scratch_shapes=[
                pltpu.VMEM((2, SLOTS, 1024), jnp.bfloat16),
                pltpu.SemaphoreType.DMA((2, 4)),
            ],
        ),
        out_shape=jax.ShapeDtypeStruct((NDP, 2, 2, H, UNIT), jnp.bfloat16),
        compiler_params=params(),
        cost_estimate=cost(2 * 2 * SLOTS * H * 2048, 2 * SLOTS * 2048 * 2 + 2 * H * 2048 * 2),
        name=f"partial{chunk}",
    )(where, weighted, *buffers)


def grads_kernel(where_ref, factor_ref, gate_ref, up_ref, weight_ref, effective_ref, *refs):
    buffers = refs[: 8 * CHUNKS]
    gate_out, up_out, score_out, rows, eff, turned, total, sems = refs[8 * CHUNKS :]
    step = pl.program_id(0)
    slot = step & 1
    e = step // 4
    part = step & 3

    def copies(at_e, i, into):
        group, chunk = i // 2, i % 2
        quarter = where_ref[8 + group] * 2 + chunk
        return row_copies(
            where_ref, buffers[8 * chunk : 8 * chunk + 8], group, at_e, rows.at[into], sems.at[into]
        ) + [
            pltpu.make_async_copy(
                effective_ref.at[j, quarter, at_e],
                eff.at[into, :, pl.ds(j * UNIT, UNIT)],
                sems.at[into, 4 + j],
            )
            for j in range(NDP)
        ]

    def fetch(at, into):
        for i in range(4):
            @pl.when((at & 3) == i)
            def _(i=i):
                for copy in copies(at // 4, i, into):
                    copy.start()

    @pl.when(step == 0)
    def _():
        fetch(step, 0)

    @pl.when(step < 7)
    def _():
        fetch(step + 1, 1 - slot)

    for copy in copies(0, 0, slot):
        copy.wait()

    half = where_ref[8 + part // 2]
    first = (part & 1) == 0

    def add(target):
        for n in range(H // 256):
            value = lax.dot_general(
                rows[slot],
                eff[slot, n * 256 : (n + 1) * 256, :],
                (((1,), (1,)), ((), ())),
                preferred_element_type=jnp.float32,
            )
            columns = slice(n * 256, (n + 1) * 256)

            @pl.when(first)
            def _(value=value, columns=columns):
                target[:, columns] = value

            @pl.when(jnp.logical_not(first))
            def _(value=value, columns=columns):
                target[:, columns] += value

    @pl.when(half == 0)
    def _():
        add(turned)

    @pl.when(half == 1)
    def _():
        add(total)

    @pl.when(part == 3)
    def _():
        factor = factor_ref[e]

        def piece(i, carry):
            at = pl.ds(pl.multiple_of(i * 2 * PART, 2 * PART), 2 * PART)
            zz = i // 2
            xx = (i - zz * 2) * 2
            one = pl.ds(pl.multiple_of((xx * NZ + zz) * PART, PART), PART)
            two = pl.ds(pl.multiple_of(((xx + 1) * NZ + zz) * PART, PART), PART)
            slot_grads = factor * (
                total[at, :] + jnp.concatenate([turned[one, :], turned[two, :]], axis=0)
            )
            gate = gate_ref[0, at, :].astype(jnp.float32)
            up = up_ref[0, at, :].astype(jnp.float32)
            sig = 1.0 / (1.0 + jnp.exp(-gate))
            activated = gate * sig
            score_out[0, at, :] = jnp.sum(slot_grads * (activated * up), axis=1, keepdims=True)
            scaled = weight_ref[0, at, :] * slot_grads
            gate_out[0, at, :] = (scaled * up * sig * (1.0 + gate * (1.0 - sig))).astype(
                jnp.bfloat16
            )
            up_out[0, at, :] = (scaled * activated).astype(jnp.bfloat16)
            return carry

        lax.fori_loop(0, SLOTS // (2 * PART), piece, 0)


def grads(where, factor, gate, up, slot_weight, effective, buffers):
    any_spec = pl.BlockSpec(memory_space=pl.ANY)
    whole = pl.BlockSpec((1, SLOTS, H), lambda n, s, f: (n // 4, 0, 0))
    column = pl.BlockSpec((1, SLOTS, 1), lambda n, s, f: (n // 4, 0, 0))
    return pl.pallas_call(
        grads_kernel,
        grid_spec=pltpu.PrefetchScalarGridSpec(
            num_scalar_prefetch=2,
            grid=(8,),
            in_specs=[whole, whole, column, any_spec] + [any_spec] * (8 * CHUNKS),
            out_specs=[whole, whole, column],
            scratch_shapes=[
                pltpu.VMEM((2, SLOTS, 1024), jnp.bfloat16),
                pltpu.VMEM((2, H, 1024), jnp.bfloat16),
                pltpu.VMEM((SLOTS, H), jnp.float32),
                pltpu.VMEM((SLOTS, H), jnp.float32),
                pltpu.SemaphoreType.DMA((2, 8)),
            ],
        ),
        out_shape=[
            jax.ShapeDtypeStruct((2, SLOTS, H), jnp.bfloat16),
            jax.ShapeDtypeStruct((2, SLOTS, H), jnp.bfloat16),
            jax.ShapeDtypeStruct((2, SLOTS, 1), jnp.float32),
        ],
        compiler_params=params(),
        cost_estimate=cost(2 * 2 * SLOTS * H * D, 2 * SLOTS * D * 2 + 2 * H * D * 2, 2 * SLOTS * H),
        name="grads",
    )(where, factor, gate, up, slot_weight, effective, *buffers)


def on_device(grad_out, expert_ids, route_weights, gate_values, up_values, w_down):
    me = lax.axis_index("expert")
    core = me % 2
    x = (me // 2) % NX
    z = me // (2 * NX)
    move = lambda value, *to: lax.ppermute(value, "expert", pairs(*to))

    halves = grad_out.reshape(TOK, NDP, 2, CHUNKS, UNIT).transpose(2, 3, 0, 1, 4)
    halves = halves.reshape(2, CHUNKS, TOK, 1024)
    mine = lax.dynamic_index_in_dim(halves, core, 0, keepdims=False)
    theirs = lax.dynamic_index_in_dim(halves, 1 - core, 0, keepdims=False)
    partner = move(theirs, True, 0, 1)
    block = jnp.where(
        core == 0, jnp.stack([mine, partner], axis=1), jnp.stack([partner, mine], axis=1)
    ).reshape(CHUNKS, 2 * TOK, 1024)
    blocks = [block] + [move(block, True, shift, 0) for shift in SHIFTS[1:]]

    shrunk, sums = shrink(w_down)
    effective = lax.all_gather(shrunk, "dp", axis=0)
    sums = lax.psum(jnp.sum(sums, axis=(0, 3, 4)), "dp")
    factor = sums[:, 0] / (sums[:, 1] + epsilon)

    table, rank = route(expert_ids, route_weights)
    tables = lax.all_gather(table, "expert", axis=0)
    slot_weight = lax.dynamic_slice_in_dim(tables[:, :, TOK : TOK + CAP], 2 * me, 2, 1)
    slot_weight = slot_weight.astype(jnp.float32).transpose(1, 0, 2).reshape(2, SLOTS, 1)

    ranks = tables[:, :, :TOK].reshape(NZ, NX, 2, 64, TOK)
    ranks = jnp.where(
        core == 0,
        lax.dynamic_index_in_dim(ranks, x, 1, keepdims=False),
        lax.dynamic_index_in_dim(ranks, z, 0, keepdims=False),
    ).reshape(4, 2, NZ, NX, 2, 2, TOK)
    ranks = jnp.where(
        core == 0,
        lax.dynamic_index_in_dim(ranks, z, 2, keepdims=False),
        lax.dynamic_index_in_dim(ranks, x, 3, keepdims=False),
    )
    place = jnp.where(core == 0, x, z)
    ranks = jnp.stack(
        [
            lax.dynamic_index_in_dim(ranks, (place + shift) % 4, 2, keepdims=False)
            for shift in SHIFTS
        ],
        axis=2,
    )
    ranks = jnp.where(core == 0, ranks, ranks[:, :, :, ::-1])
    ranks = ranks.transpose(0, 2, 3, 4, 1, 5).reshape(4, 16, 2 * TOK).astype(jnp.float32)

    shifts = jnp.array(SHIFTS, jnp.int32)
    held = jnp.where(core == 0, z, x)
    held = ((held - shifts) % 4).astype(jnp.int32)

    gate, up = gate_values[0], up_values[0]
    weighted = weigh(gate, up, slot_weight)

    same = (jnp.where(core == 0, x, z) - shifts) % 4
    other = (jnp.where(core == 0, z, x) - shifts) % 4
    where = jnp.concatenate([same, other, jnp.stack([core, 1 - core])]).astype(jnp.int32)

    buffers, summed = [], []
    for chunk in range(CHUNKS):
        rows = pick(chunk, held, ranks, blocks)
        got = [
            rows[2 * i + swap]
            if i == 0 and swap == 0
            else move(rows[2 * i + swap], False, shift, swap)
            for swap in range(2)
            for i, shift in enumerate(SHIFTS)
        ]
        buffers += got
        part = partial(chunk, where, weighted, got)
        summed.append(lax.psum_scatter(part, "dp", scatter_dimension=0, tiled=False))

    grad_gate, grad_up, scores = grads(where, factor, gate, up, slot_weight, effective, buffers)
    returned = lax.all_to_all(
        scores.reshape(2, SLOTS), "expert", split_axis=1, concat_axis=0, tiled=True
    )
    grad_route = back(expert_ids, rank, returned)

    summed = jnp.stack(summed, axis=1)
    summed = summed.transpose(2, 3, 0, 1, 4).reshape(2, H, 1024)
    grad_down = (factor[:, None, None] * summed.astype(jnp.float32)).astype(jnp.bfloat16)
    return (grad_gate[None], grad_up[None], grad_down, grad_route)


def solution(mesh):
    in_specs = (
        P(("dp", "expert"), None),
        P(("dp", "expert"), None),
        P(("dp", "expert"), None),
        P("dp", "expert", None, None),
        P("dp", "expert", None, None),
        P("expert", None, "dp"),
    )
    out_specs = (
        P("dp", "expert", None, None),
        P("dp", "expert", None, None),
        P("expert", None, "dp"),
        P(("dp", "expert"), None),
    )
    return jax.shard_map(
        on_device, mesh=mesh, in_specs=in_specs, out_specs=out_specs, check_vma=False
    )
```

time: 850 us -> 512 us (0.60)
  waiting for transfers between devices: 429 us -> 275 us
  matrix products: 136 us -> 0 us
  local copies, waits for them, and re-layouts: 163 us -> 27.7 us
  Pallas kernels: 0 us -> 120 us
  other arithmetic: 71.1 us -> 14.2 us
  starting transfers between devices: 24.6 us -> 49.9 us
    all_to_all x3 -> x1, waiting for transfers between devices: 241 us -> 1.02 us  [on_device(): lax.all_to_all(scores.reshape(2, SLOTS), 'expert', split_axis=1, concat_a...]
    dot_general x2 -> x0, matrix products: 136 us -> none  [the longest x1 91.9 us: on_device(): jnp.einsum('esh,esd->ehd', weighted, arrived, preferred_element_type=jnp....]
    pallas_call x0 -> x9, Pallas kernels: none -> 120 us  [the longest x1 45.8 us: grads(): pl.pallas_call(grads_kernel, grid_spec=pltpu.PrefetchScalarGridSpec(num_s...]
    ppermute x0 -> x18, waiting for transfers between devices: none -> 93.6 us  [on_device(): move = lambda value, *to: lax.ppermute(value, 'expert', pairs(*to))]
    gather x4 -> x0, local copies, waits for them, and re-layouts: 64.1 us -> none  [the longest x2 38.4 us: on_device(): grad_out[source_row // top_count]]
    ppermute x0 -> x18, starting transfers between devices: none -> 42 us  [on_device(): move = lambda value, *to: lax.ppermute(value, 'expert', pairs(*to))]
    all_to_all x4 -> x2, local copies, waits for them, and re-layouts: 35.8 us -> 0.75 us  [on_device(): lax.all_to_all(scores.reshape(2, SLOTS), 'expert', split_axis=1, concat_a...]
    reduce_scatter x1 -> x2, waiting for transfers between devices: 69.9 us -> 41.7 us  [on_device(): lax.psum_scatter(part, 'dp', scatter_dimension=0, tiled=False)]
  transfers between devices with their start and end apart: 5 -> 23, of which waited for: 3 -> 11; matrix products, arithmetic and copies ran while one was open for 15% -> 7% of each run, Pallas kernels for 0% -> 9%
where the time goes in v1:
time: 512 us; the launch traced here: 511 us
  waiting for transfers between devices  275 us (54%)
  Pallas kernels  120 us (23%)
  starting transfers between devices  49.9 us (10%)
  local copies, waits for them, and re-layouts  27.7 us (5%)
  other arithmetic  14.2 us (3%)
  between operations  14.1 us (3%)
  blocking collectives  9.66 us (2%)
    all_gather x1, waiting for transfers between devices, on_device(): effective = lax.all_gather(shrunk, 'dp', axis=0)  109 us
    ppermute x18, waiting for transfers between devices, on_device(): move = lambda value, *to: lax.ppermute(value, 'expert', pairs(*to))  93.6 us
    pallas_call x1, Pallas kernels, grads(): pl.pallas_call(grads_kernel, grid_spec=pltpu.PrefetchScalarGridSpec(num_s...  45.8 us
    ppermute x18, starting transfers between devices, on_device(): move = lambda value, *to: lax.ppermute(value, 'expert', pairs(*to))  42 us
    reduce_scatter x2, waiting for transfers between devices, on_device(): lax.psum_scatter(part, 'dp', scatter_dimension=0, tiled=False)  41.7 us
    all_gather x1, waiting for transfers between devices, on_device(): tables = lax.all_gather(table, 'expert', axis=0)  30.1 us
    pallas_call x2, Pallas kernels, partial(): pl.pallas_call(partial_kernel, grid_spec=pltpu.PrefetchScalarGridSpec(num...  29.3 us
    pallas_call x2, Pallas kernels, pick(): pl.pallas_call(functools.partial(pick_kernel, chunk), grid_spec=pltpu.Pre...  21.6 us
  transfers between devices with their start and end apart: 23, of which 11 were waited for; matrix products, arithmetic and copies ran while one was open for 7% of the time, Pallas kernels for 9%

profile of v1, /device:TPU:1, one launch (start us, length us, event | category | flops | bytes accessed | tf_op | source)
XLA Modules:
  0.0 510.8 jit_solution(12621192136753221394)
XLA Ops:
  7.2 1.3 convert_bitcast_fusion.3.weights_ref
  8.5 1.9 route.1
  10.5 4.1 copy.49
  14.5 1.7 copy.50
  16.3 1.1 constant_dynamic-slice_fusion.1
  17.4 2.3 copy.52
  19.7 1.4 collective-permute-start
  21.6 2.0 collective-permute-done
  24.1 1.4 collective-permute-start.1
  25.5 1.4 collective-permute-start.2
  26.9 1.6 collective-permute-start.3
  29.1 30.1 %all-gather.5.cloned.1.call-done = bf16[2048,384]{1,0:T(8,128)(2,1)} async-done(((bf16[64,384]{1,0:T(8,128)(2,1)}), bf16[2048,384]{1,0:T(8,128)(2,1)}) %all-gather.5.cloned.1.call-update) | async-done | bytes 1572880 | tf_op jit(solution)/shard_map/all_gather | solution.py:470
  59.2 1.3 slice.17
  62.5 15.4 %collective-permute-done.3.refs_3_ = bf16[2,512,1024]{2,1,0:T(8,128)(2,1)} collective-permute-done((bf16[2,512,1024]{2,1,0:T(8,128)(2,1)S(1)}, bf16[2,512,1024]{2,1,0:T(8,128)(2,1)}, u32[]{:S(2)}, u32[]{:S(2)}) %collective-permute-start.3) | collective-permute-done | bytes 2097184 | tf_op jit(solution)/shard_map/ppermute | solution.py:452
  77.9 10.9 %pick1.1 = (bf16[2,288,1024]{2,1,0:T(8,128)(2,1)}, bf16[2,288,1024]{2,1,0:T(8,128)(2,1)}, bf16[2,288,1024]{2,1,0:T(8,128)(2,1)}, bf16[2,288,1024]{2,1,0:T(8,128)...) custom-call(s32[4]{0:T(128)} %get-tuple-element.73.where_ref, ...), custom_call_target="tpu_custom_call" | custom-call | flops 4831838208 | bytes 13631488 | tf_op jit(solution)/shard_map/pick1/pallas_call | solution.py:199
  88.8 1.4 collective-permute-start.11
  90.2 7.0 %collective-permute-start.12 = (bf16[2,288,1024]{2,1,0:T(8,128)(2,1)}, bf16[2,288,1024]{2,1,0:T(8,128)(2,1)S(1)}, u32[]{:S(2)}, u32[]{:S(2)}) collective-permute-start(bf16[2,288,1024]{2,1,0:T(8,128)(2,1)} %get-tuple-element.40), channel_id=1, source_target_pairs={{0,6},{1,25},{2,0},{3,27},{4,2},{5,29},{6,4},{7,31},{8,14},{9,1},{... | collective-permute-start | bytes 3538952 | tf_op jit(solution)/shard_map/ppermute | solution.py:452
  97.2 1.1 collective-permute-start.13
  98.3 1.3 collective-permute-start.15
  99.5 11.4 %collective-permute-done.11.refs_9_.refs_1_ = bf16[2,288,1024]{2,1,0:T(8,128)(2,1)S(1)} collective-permute-done((bf16[2,288,1024]{2,1,0:T(8,128)(2,1)}, bf16[2,288,1024]{2,1,0:T(8,128)(2,1)S(1)}, u32[]{:S(2)}, u32[]{:S(2)}) %collective-permute-start.11) | collective-permute-done | bytes 1179680 | tf_op jit(solution)/shard_map/ppermute | solution.py:452
  110.9 16.6 %collective-permute-start.16 = (bf16[2,288,1024]{2,1,0:T(8,128)(2,1)}, bf16[2,288,1024]{2,1,0:T(8,128)(2,1)}, u32[]{:S(2)}, u32[]{:S(2)}) collective-permute-start(bf16[2,288,1024]{2,1,0:T(8,128)(2,1)} %get-tuple-element.44), channel_id=1, source_target_pairs={{0,7},{1,24},{2,1},{3,26},{4,3},{5,28},{6,5},{7,30},{8,15},{9,0},{... | collective-permute-start | bytes 3538952 | tf_op jit(solution)/shard_map/ppermute | solution.py:452
  128.2 1.1 slice.16
  129.3 1.4 reshape.67.weight_ref
  130.7 9.1 %weigh.1.weighted_ref = bf16[2,2,768,1152]{3,2,1,0:T(8,128)(2,1)} custom-call(bf16[2,1152,768]{2,1,0:T(8,128)(2,1)} %bitcast.45, bf16[2,1152,768]{2,1,0:T(8,128)(2,1)} %bitcast.47, f32[2,1152,1]{2,1,0:T(8,128)} %reshape.67.weight_ref), custom_call_target="tpu_custom_call" | custom-call | flops 35389440 | bytes 14155776 | tf_op jit(solution)/shard_map/weigh/pallas_call | solution.py:239
  139.8 13.7 %collective-permute-done.16.refs_14_.refs_6_ = bf16[2,288,1024]{2,1,0:T(8,128)(2,1)} collective-permute-done((bf16[2,288,1024]{2,1,0:T(8,128)(2,1)}, bf16[2,288,1024]{2,1,0:T(8,128)(2,1)}, u32[]{:S(2)}, u32[]{:S(2)}) %collective-permute-start.16) | collective-permute-done | bytes 1179680 | tf_op jit(solution)/shard_map/ppermute | solution.py:452
  153.6 14.6 %partial1.1 = bf16[4,2,2,768,256]{4,3,2,1,0:T(8,128)(2,1)} custom-call(s32[10]{0:T(128)} %pad_add_fusion.where_ref, bf16[2,2,768,1152]{3,2,1,0:T(8,128)(2,1)} %weigh.1.weighted_ref, bf16[2,288,1024]{2,1,0:T(8,128)(2,1)} %get-tuple-element.38.refs_8_.refs_0_, bf16[2,288,1024]{2,1,0:T(8,128)(2,1)} %copy-done.6, bf16[2,288,1024]{2,1,0:T(8,128)(2,1)} %copy-done.7, ...), custom_call_target="tpu_custom_call" | custom-call | flops 7247757312 | bytes 15728640 | tf_op jit(solution)/shard_map/partial1/pallas_call | solution.py:298
  168.3 10.7 %pick0.1 = (bf16[2,288,1024]{2,1,0:T(8,128)(2,1)}, bf16[2,288,1024]{2,1,0:T(8,128)(2,1)}, bf16[2,288,1024]{2,1,0:T(8,128)(2,1)}, bf16[2,288,1024]{2,1,0:T(8,128)...) custom-call(s32[4]{0:T(128)} %get-tuple-element.73.where_ref, ...), custom_call_target="tpu_custom_call" | custom-call | flops 4831838208 | bytes 13631488 | tf_op jit(solution)/shard_map/pick0/pallas_call | solution.py:199
  179.1 2.7 collective-permute-start.5
  181.8 1.7 collective-permute-start.8
  183.5 25.1 %collective-permute-done.4.refs_1_ = bf16[2,288,1024]{2,1,0:T(8,128)(2,1)S(1)} collective-permute-done((bf16[2,288,1024]{2,1,0:T(8,128)(2,1)}, bf16[2,288,1024]{2,1,0:T(8,128)(2,1)S(1)}, u32[]{:S(2)}, u32[]{:S(2)}) %collective-permute-start.4) | collective-permute-done | bytes 1179680 | tf_op jit(solution)/shard_map/ppermute | solution.py:452
  208.6 4.5 collective-permute-start.9
  213.1 18.4 %collective-permute-done.8.refs_5_ = bf16[2,288,1024]{2,1,0:T(8,128)(2,1)S(1)} collective-permute-done((bf16[2,288,1024]{2,1,0:T(8,128)(2,1)}, bf16[2,288,1024]{2,1,0:T(8,128)(2,1)S(1)}, u32[]{:S(2)}, u32[]{:S(2)}) %collective-permute-start.8) | collective-permute-done | bytes 1179680 | tf_op jit(solution)/shard_map/ppermute | solution.py:452
  231.5 7.7 %collective-permute-done.9.refs_6_ = bf16[2,288,1024]{2,1,0:T(8,128)(2,1)S(1)} collective-permute-done((bf16[2,288,1024]{2,1,0:T(8,128)(2,1)}, bf16[2,288,1024]{2,1,0:T(8,128)(2,1)S(1)}, u32[]{:S(2)}, u32[]{:S(2)}) %collective-permute-start.9) | collective-permute-done | bytes 1179680 | tf_op jit(solution)/shard_map/ppermute | solution.py:452
  239.2 1.0 copy-done.13
  240.2 14.6 %partial0.1 = bf16[4,2,2,768,256]{4,3,2,1,0:T(8,128)(2,1)} custom-call(s32[10]{0:T(128)} %pad_add_fusion.where_ref, bf16[2,2,768,1152]{3,2,1,0:T(8,128)(2,1)} %weigh.1.weighted_ref, bf16[2,288,1024]{2,1,0:T(8,128)(2,1)} %get-tuple-element.30.refs_0_, bf16[2,288,1024]{2,1,0:T(8,128)(2,1)} %copy-done.8, bf16[2,288,1024]{2,1,0:T(8,128)(2,1)} %copy-done.9, ...), custom_call_target="tpu_custom_call" | custom-call | flops 7247757312 | bytes 15728640 | tf_op jit(solution)/shard_map/partial0/pallas_call | solution.py:298
  254.9 10.4 %shrink.1 = (bf16[4,2,768,256]{3,2,1,0:T(8,128)(2,1)}, f32[4,2,2,8,128]{4,3,2,1,0:T(8,128)}) custom-call(bf16[2,768,1024]{2,1,0:T(8,128)(2,1)} %w_ref.1), custom_call_target="tpu_custom_call" | custom-call | flops 47185920 | bytes 6291456 | tf_op jit(solution)/shard_map/shrink/pallas_call | solution.py:81
  266.2 9.7 %psum.7 = f32[2,2]{1,0:T(2,128)S(1)} all-reduce(f32[2,2]{1,0:T(2,128)S(1)} %reduce_sum.9), channel_id=1, replica_groups=mesh['dp'=4,'expert'=32] {'dp'}, use_global_device_ids=true, to_apply=%region_1.2 | all-reduce | flops 4 | bytes 32 | tf_op jit(solution)/shard_map/psum | solution.py:466
  276.6 41.7 %reduce-scatter.3.cloned.1.call-done = bf16[1,2,2,768,256]{4,3,2,1,0:T(8,128)(2,1)} async-done(((bf16[4,2,2,768,256]{4,3,2,1,0:T(8,128)(2,1)}), bf16[1,2,2,768,256]{4,3,2,1,0:T(8,128)(2,1)}) %reduce-scatter.3.cloned.1.call-update) | async-done | bytes 1572880 | tf_op jit(solution)/shard_map/reduce_scatter | solution.py:519
  318.3 4.9 convert_bitcast_fusion
  323.2 6.6 %copy.56 = f32[2,768,2,2,256]{1,4,3,2,0:T(8,128)} copy(f32[2,768,2,2,256]{4,1,0,2,3:T(8,128)} %convert_bitcast_fusion) | data formatting | bytes 12582912 | tf_op jit(solution)/shard_map/convert_element_type | solution.py:529
  329.8 108.6 %all-gather.7.cloned.1.call-done = bf16[16,2,768,256]{3,2,1,0:T(8,128)(2,1)} async-done(((bf16[4,2,768,256]{3,2,1,0:T(8,128)(2,1)}), bf16[16,2,768,256]{3,2,1,0:T(8,128)(2,1)}) %all-gather.7.cloned.1.call-update) | async-done | bytes 12582928 | tf_op jit(solution)/shard_map/all_gather | solution.py:465
  438.5 45.8 %grads.1 = (bf16[2,1152,768]{2,1,0:T(8,128)(2,1)}, bf16[2,1152,768]{2,1,0:T(8,128)(2,1)}, f32[2,1152,1]{2,1,0:T(8,128)}) custom-call(s32[10]{0:T(128)} %pad_add_fusion.where_ref, f32[2]{0:T(128)} %fusion.1.factor_ref, bf16[2,1152,768]{2,1,0:T(8,128)(2,1)} %bitcast.46, bf16[2,1152,768]{2,1,0:T(8,128)(2,1)} %bitcast.48, f32[2,1152,1]{2,1,0:T(8,128)} %reshape.67.weight_ref, ...), custom_call_target="tpu_custom_call" | custom-call | flops 14495514624 | bytes 31457280 | tf_op jit(solution)/shard_map/grads/pallas_call | solution.py:421
  484.3 1.7 reduce.1
  486.7 7.7 %all-to-all-start = ((f32[2,32,36]{2,0,1:T(2,128)}), f32[2,32,36]{2,0,1:T(2,128)S(1)}, u32[]{:S(2)}, u32[]{:S(2)}) async-start(f32[2,32,36]{2,0,1:T(2,128)} %copy.57), calls=%async_computation.2 | async-start | bytes 65536 | tf_op jit(solution)/shard_map/all_to_all | solution.py:522
  494.4 3.3 fusion
  497.8 2.9 copy.58
  500.6 1.0 all-to-all-done
  502.3 2.0 back.1
  (74 shorter events, 7.7 us)
Async XLA Ops:
  7.2 52.1 %all-gather.5.cloned.1.call-start = ((), (), s32[]{:S(2)}) async-start(), calls=%async_computation.5 | async-start | bytes 1622016 | tf_op jit(solution)/shard_map/all_gather | solution.py:470
  10.4 266.2 %reduce-scatter.5.cloned.1.call-start = ((), (), s32[]{:S(2)}) async-start(), calls=%async_computation.4 | async-start | bytes 7864320 | tf_op jit(solution)/shard_map/reduce_scatter | solution.py:519
  19.7 3.9 collective-permute-start
  23.9 4.6 copy-start.5
  24.1 37.1 %copy-start = (bf16[2,2,256,1024]{3,2,1,0:T(8,128)(2,1)}, bf16[2,2,256,1024]{3,2,1,0:T(8,128)(2,1)S(1)}, u32[]{:S(2)}) copy-start(bf16[2,2,256,1024]{3,2,1,0:T(8,128)(2,1)S(1)} %copy.53) | copy-start | bytes 6291460
  24.1 38.4 %collective-permute-start.1 = (bf16[2,512,1024]{2,1,0:T(8,128)(2,1)S(1)}, bf16[2,512,1024]{2,1,0:T(8,128)(2,1)}, u32[]{:S(2)}, u32[]{:S(2)}) collective-permute-start(bf16[2,512,1024]{2,1,0:T(8,128)(2,1)S(1)} %bitcast.51), channel_id=1, source_target_pairs={{0,8},{1,3},{2,10},{3,5},{4,12},{5,7},{6,14},{7,1},{8,16},{9,11},{... | collective-permute-start | bytes 6291464 | tf_op jit(solution)/shard_map/ppermute | solution.py:452
  25.5 37.1 %collective-permute-start.2 = (bf16[2,512,1024]{2,1,0:T(8,128)(2,1)S(1)}, bf16[2,512,1024]{2,1,0:T(8,128)(2,1)}, u32[]{:S(2)}, u32[]{:S(2)}) collective-permute-start(bf16[2,512,1024]{2,1,0:T(8,128)(2,1)S(1)} %bitcast.52), channel_id=1, source_target_pairs={{0,24},{1,7},{2,26},{3,1},{4,28},{5,3},{6,30},{7,5},{8,0},{9,15},{... | collective-permute-start | bytes 6291464 | tf_op jit(solution)/shard_map/ppermute | solution.py:452
  26.9 51.0 %collective-permute-start.3 = (bf16[2,512,1024]{2,1,0:T(8,128)(2,1)S(1)}, bf16[2,512,1024]{2,1,0:T(8,128)(2,1)}, u32[]{:S(2)}, u32[]{:S(2)}) collective-permute-start(bf16[2,512,1024]{2,1,0:T(8,128)(2,1)S(1)} %bitcast.53), channel_id=1, source_target_pairs={{0,16},{1,5},{2,18},{3,7},{4,20},{5,1},{6,22},{7,3},{8,24},{9,13},... | collective-permute-start | bytes 6291464 | tf_op jit(solution)/shard_map/ppermute | solution.py:452
  77.9 49.6 %copy-start.4 = (s32[4]{0:T(128)S(1)}, s32[4]{0:T(128)}, u32[]{:S(2)}) copy-start(s32[4]{0:T(128)} %get-tuple-element.73.where_ref) | copy-start | bytes 52
  88.8 22.1 %collective-permute-start.11 = (bf16[2,288,1024]{2,1,0:T(8,128)(2,1)}, bf16[2,288,1024]{2,1,0:T(8,128)(2,1)S(1)}, u32[]{:S(2)}, u32[]{:S(2)}) collective-permute-start(bf16[2,288,1024]{2,1,0:T(8,128)(2,1)} %get-tuple-element.39), channel_id=1, source_target_pairs={{0,2},{1,9},{2,4},{3,11},{4,6},{5,13},{6,0},{7,15},{8,10},{9,17},{... | collective-permute-start | bytes 3538952 | tf_op jit(solution)/shard_map/ppermute | solution.py:452
  90.2 37.3 %collective-permute-start.12 = (bf16[2,288,1024]{2,1,0:T(8,128)(2,1)}, bf16[2,288,1024]{2,1,0:T(8,128)(2,1)S(1)}, u32[]{:S(2)}, u32[]{:S(2)}) collective-permute-start(bf16[2,288,1024]{2,1,0:T(8,128)(2,1)} %get-tuple-element.40), channel_id=1, source_target_pairs={{0,6},{1,25},{2,0},{3,27},{4,2},{5,29},{6,4},{7,31},{8,14},{9,1},{... | collective-permute-start | bytes 3538952 | tf_op jit(solution)/shard_map/ppermute | solution.py:452
  97.2 42.7 %collective-permute-start.13 = (bf16[2,288,1024]{2,1,0:T(8,128)(2,1)}, bf16[2,288,1024]{2,1,0:T(8,128)(2,1)}, u32[]{:S(2)}, u32[]{:S(2)}) collective-permute-start(bf16[2,288,1024]{2,1,0:T(8,128)(2,1)} %get-tuple-element.41), channel_id=1, source_target_pairs={{0,4},{1,17},{2,6},{3,19},{4,0},{5,21},{6,2},{7,23},{8,12},{9,25},... | collective-permute-start | bytes 3538952 | tf_op jit(solution)/shard_map/ppermute | solution.py:452
  98.3 41.6 %collective-permute-start.14 = (bf16[2,288,1024]{2,1,0:T(8,128)(2,1)}, bf16[2,288,1024]{2,1,0:T(8,128)(2,1)}, u32[]{:S(2)}, u32[]{:S(2)}) collective-permute-start(bf16[2,288,1024]{2,1,0:T(8,128)(2,1)} %get-tuple-element.42), channel_id=1, source_target_pairs={{0,1},{1,0},{2,3},{3,2},{4,5},{5,4},{6,7},{7,6},{8,9},{9,8},{10,11... | collective-permute-start | bytes 3538952 | tf_op jit(solution)/shard_map/ppermute | solution.py:452
  98.3 41.6 %collective-permute-start.15 = (bf16[2,288,1024]{2,1,0:T(8,128)(2,1)}, bf16[2,288,1024]{2,1,0:T(8,128)(2,1)}, u32[]{:S(2)}, u32[]{:S(2)}) collective-permute-start(bf16[2,288,1024]{2,1,0:T(8,128)(2,1)} %get-tuple-element.43), channel_id=1, source_target_pairs={{0,3},{1,8},{2,5},{3,10},{4,7},{5,12},{6,1},{7,14},{8,11},{9,16},{... | collective-permute-start | bytes 3538952 | tf_op jit(solution)/shard_map/ppermute | solution.py:452
  110.9 28.9 %copy-start.6 = (bf16[2,288,1024]{2,1,0:T(8,128)(2,1)}, bf16[2,288,1024]{2,1,0:T(8,128)(2,1)S(1)}, u32[]{:S(2)}) copy-start(bf16[2,288,1024]{2,1,0:T(8,128)(2,1)S(1)} %collective-permute-done.11.refs_9_.refs_1_) | copy-start | bytes 3538948
  110.9 42.7 %collective-permute-start.16 = (bf16[2,288,1024]{2,1,0:T(8,128)(2,1)}, bf16[2,288,1024]{2,1,0:T(8,128)(2,1)}, u32[]{:S(2)}, u32[]{:S(2)}) collective-permute-start(bf16[2,288,1024]{2,1,0:T(8,128)(2,1)} %get-tuple-element.44), channel_id=1, source_target_pairs={{0,7},{1,24},{2,1},{3,26},{4,3},{5,28},{6,5},{7,30},{8,15},{9,0},{... | collective-permute-start | bytes 3538952 | tf_op jit(solution)/shard_map/ppermute | solution.py:452
  127.5 12.3 %copy-start.7 = (bf16[2,288,1024]{2,1,0:T(8,128)(2,1)}, bf16[2,288,1024]{2,1,0:T(8,128)(2,1)S(1)}, u32[]{:S(2)}) copy-start(bf16[2,288,1024]{2,1,0:T(8,128)(2,1)S(1)} %collective-permute-done.12.refs_10_.refs_2_) | copy-start | bytes 3538948
  127.5 26.1 %collective-permute-start.17 = (bf16[2,288,1024]{2,1,0:T(8,128)(2,1)}, bf16[2,288,1024]{2,1,0:T(8,128)(2,1)}, u32[]{:S(2)}, u32[]{:S(2)}) collective-permute-start(bf16[2,288,1024]{2,1,0:T(8,128)(2,1)} %get-tuple-element.45), channel_id=1, source_target_pairs={{0,5},{1,16},{2,7},{3,18},{4,1},{5,20},{6,3},{7,22},{8,13},{9,24},... | collective-permute-start | bytes 3538952 | tf_op jit(solution)/shard_map/ppermute | solution.py:452
  168.2 150.1 %reduce-scatter.3.cloned.1.call-start = ((), (), s32[]{:S(2)}) async-start(), calls=%async_computation.3 | async-start | bytes 7864320 | tf_op jit(solution)/shard_map/reduce_scatter | solution.py:519
  179.0 29.6 %collective-permute-start.4 = (bf16[2,288,1024]{2,1,0:T(8,128)(2,1)}, bf16[2,288,1024]{2,1,0:T(8,128)(2,1)S(1)}, u32[]{:S(2)}, u32[]{:S(2)}) collective-permute-start(bf16[2,288,1024]{2,1,0:T(8,128)(2,1)} %get-tuple-element.31), channel_id=1, source_target_pairs={{0,2},{1,9},{2,4},{3,11},{4,6},{5,13},{6,0},{7,15},{8,10},{9,17},{... | collective-permute-start | bytes 3538952 | tf_op jit(solution)/shard_map/ppermute | solution.py:452
  179.1 34.0 %collective-permute-start.5 = (bf16[2,288,1024]{2,1,0:T(8,128)(2,1)}, bf16[2,288,1024]{2,1,0:T(8,128)(2,1)S(1)}, u32[]{:S(2)}, u32[]{:S(2)}) collective-permute-start(bf16[2,288,1024]{2,1,0:T(8,128)(2,1)} %get-tuple-element.32), channel_id=1, source_target_pairs={{0,6},{1,25},{2,0},{3,27},{4,2},{5,29},{6,4},{7,31},{8,14},{9,1},{... | collective-permute-start | bytes 3538952 | tf_op jit(solution)/shard_map/ppermute | solution.py:452
  181.8 31.3 %collective-permute-start.6 = (bf16[2,288,1024]{2,1,0:T(8,128)(2,1)}, bf16[2,288,1024]{2,1,0:T(8,128)(2,1)S(1)}, u32[]{:S(2)}, u32[]{:S(2)}) collective-permute-start(bf16[2,288,1024]{2,1,0:T(8,128)(2,1)} %get-tuple-element.33), channel_id=1, source_target_pairs={{0,4},{1,17},{2,6},{3,19},{4,0},{5,21},{6,2},{7,23},{8,12},{9,25},... | collective-permute-start | bytes 3538952 | tf_op jit(solution)/shard_map/ppermute | solution.py:452
  181.8 31.3 %collective-permute-start.7 = (bf16[2,288,1024]{2,1,0:T(8,128)(2,1)}, bf16[2,288,1024]{2,1,0:T(8,128)(2,1)S(1)}, u32[]{:S(2)}, u32[]{:S(2)}) collective-permute-start(bf16[2,288,1024]{2,1,0:T(8,128)(2,1)} %get-tuple-element.34), channel_id=1, source_target_pairs={{0,1},{1,0},{2,3},{3,2},{4,5},{5,4},{6,7},{7,6},{8,9},{9,8},{10,11... | collective-permute-start | bytes 3538952 | tf_op jit(solution)/shard_map/ppermute | solution.py:452
  181.8 49.7 %collective-permute-start.8 = (bf16[2,288,1024]{2,1,0:T(8,128)(2,1)}, bf16[2,288,1024]{2,1,0:T(8,128)(2,1)S(1)}, u32[]{:S(2)}, u32[]{:S(2)}) collective-permute-start(bf16[2,288,1024]{2,1,0:T(8,128)(2,1)} %get-tuple-element.35), channel_id=1, source_target_pairs={{0,3},{1,8},{2,5},{3,10},{4,7},{5,12},{6,1},{7,14},{8,11},{9,16},{... | collective-permute-start | bytes 3538952 | tf_op jit(solution)/shard_map/ppermute | solution.py:452
  208.6 30.6 %copy-start.8 = (bf16[2,288,1024]{2,1,0:T(8,128)(2,1)}, bf16[2,288,1024]{2,1,0:T(8,128)(2,1)S(1)}, u32[]{:S(2)}) copy-start(bf16[2,288,1024]{2,1,0:T(8,128)(2,1)S(1)} %collective-permute-done.4.refs_1_) | copy-start | bytes 3538948
  208.6 30.6 %collective-permute-start.9 = (bf16[2,288,1024]{2,1,0:T(8,128)(2,1)}, bf16[2,288,1024]{2,1,0:T(8,128)(2,1)S(1)}, u32[]{:S(2)}, u32[]{:S(2)}) collective-permute-start(bf16[2,288,1024]{2,1,0:T(8,128)(2,1)} %get-tuple-element.36), channel_id=1, source_target_pairs={{0,7},{1,24},{2,1},{3,26},{4,3},{5,28},{6,5},{7,30},{8,15},{9,0},{... | collective-permute-start | bytes 3538952 | tf_op jit(solution)/shard_map/ppermute | solution.py:452
  213.1 26.1 %copy-start.9 = (bf16[2,288,1024]{2,1,0:T(8,128)(2,1)}, bf16[2,288,1024]{2,1,0:T(8,128)(2,1)S(1)}, u32[]{:S(2)}) copy-start(bf16[2,288,1024]{2,1,0:T(8,128)(2,1)S(1)} %collective-permute-done.5.refs_2_) | copy-start | bytes 3538948
  213.1 26.1 %collective-permute-start.10 = (bf16[2,288,1024]{2,1,0:T(8,128)(2,1)}, bf16[2,288,1024]{2,1,0:T(8,128)(2,1)}, u32[]{:S(2)}, u32[]{:S(2)}) collective-permute-start(bf16[2,288,1024]{2,1,0:T(8,128)(2,1)} %get-tuple-element.37), channel_id=1, source_target_pairs={{0,5},{1,16},{2,7},{3,18},{4,1},{5,20},{6,3},{7,22},{8,13},{9,24},... | collective-permute-start | bytes 3538952 | tf_op jit(solution)/shard_map/ppermute | solution.py:452
  213.1 26.1 %copy-start.10 = (bf16[2,288,1024]{2,1,0:T(8,128)(2,1)}, bf16[2,288,1024]{2,1,0:T(8,128)(2,1)S(1)}, u32[]{:S(2)}) copy-start(bf16[2,288,1024]{2,1,0:T(8,128)(2,1)S(1)} %collective-permute-done.6.refs_3_) | copy-start | bytes 3538948
  213.1 26.1 %copy-start.11 = (bf16[2,288,1024]{2,1,0:T(8,128)(2,1)}, bf16[2,288,1024]{2,1,0:T(8,128)(2,1)S(1)}, u32[]{:S(2)}) copy-start(bf16[2,288,1024]{2,1,0:T(8,128)(2,1)S(1)} %collective-permute-done.7.refs_4_) | copy-start | bytes 3538948
  231.5 7.7 %copy-start.12 = (bf16[2,288,1024]{2,1,0:T(8,128)(2,1)}, bf16[2,288,1024]{2,1,0:T(8,128)(2,1)S(1)}, u32[]{:S(2)}) copy-start(bf16[2,288,1024]{2,1,0:T(8,128)(2,1)S(1)} %collective-permute-done.8.refs_5_) | copy-start | bytes 3538948
  239.2 1.0 copy-start.13
  254.9 183.6 %all-gather.7.cloned.1.call-start = ((), (), s32[]{:S(2)}) async-start(), calls=%async_computation.6 | async-start | bytes 15728640 | tf_op jit(solution)/shard_map/all_gather | solution.py:465
  265.3 0.8 copy-start.2
  438.5 55.9 %copy-start.3 = (f32[2]{0:T(128)S(1)}, f32[2]{0:T(128)}, u32[]{:S(2)}) copy-start(f32[2]{0:T(128)} %fusion.1.factor_ref) | copy-start | bytes 28
  486.7 14.9 %all-to-all-start = ((f32[2,32,36]{2,0,1:T(2,128)}), f32[2,32,36]{2,0,1:T(2,128)S(1)}, u32[]{:S(2)}, u32[]{:S(2)}) async-start(f32[2,32,36]{2,0,1:T(2,128)} %copy.57), calls=%async_computation.2 | async-start | bytes 65536 | tf_op jit(solution)/shard_map/all_to_all | solution.py:522
  501.7 0.6 copy-start.1
Sparse Core Ops, SparseCore 0:
  10.8 48.3 all-gather.4
  168.3 63.2 reduce-scatter.4
  255.0 63.2 reduce-scatter.2
  320.4 118.0 all-gather.6
